TPU v7x, 512 devices: a whole 4x4x16 slice. The times are simulated.
512 devices in a mesh: slab: 128 (over x, z, core), depth: 4 (over y).
Axes of the slice: x: 4, y: 4, z: 16, core: 2. Of those that a mesh axis runs over, the one named last changes fastest.
Arguments:
- right_side: float32 [3, 8, 128, 32, 256], P(None, None, 'slab', 'depth'), may hold values from -4 to 9
- smoother: float32 [3, 128, 32, 256], P(None, 'slab', 'depth'), may hold values from 0.1 to 1
- material: int32 [128, 32, 256], P('slab', 'depth'), may hold values from 0 to 15
- moduli: float32 [16], replicated, may hold values from 0.25 to 4
- element_matrix: float32 [24, 24], replicated, may hold values from -0.15 to 3, as said below
- coarse_inverse: float32 [384, 384], replicated, may hold values from -0.2 to 1.2, as said below
- surface_map: int32 [128, 256], P('slab'), may hold values from 0 to 32767, as said below
- line_of_sight: float32 [3, 128, 256], P(None, 'slab'), may hold values from -3 to 3
Outputs:
- residual: float32 [3, 8, 128, 32, 256], P(None, None, 'slab', 'depth')
- pixels: float32 [8, 32768], P('depth', 'slab')
Inputs may be any that keep to these rules, and one draw needn't show every extreme that they name: `element_matrix`: symmetric. `coarse_inverse`: symmetric. `surface_map`: pixel p lies in tile p // 256. At most 4 surface nodes of one slab block lie in one tile, and some tile holds exactly 4 surface nodes of every slab block.
All inputs are finite; a program needn't handle non-finite values.
Results may differ from a plain program's by a relative error of at most 0.0003.
Values sent between devices are 32-bit elements; how exact they have to be, the bound alone decides.
A program may use at most 64 MiB of HBM per device.

v0:
```python
import jax
import jax.numpy as jnp
from jax import lax
from jax.sharding import PartitionSpec as P

PIX = 256


def extended(array, sides, width):
    for axis, dim in sides:
        peers, length = (lax.axis_size(axis), array.shape[dim])
        up = [(i, (i + 1) % peers) for i in range(peers - 1)]
        down = [(j, i) for i, j in up]
        last = lax.slice_in_dim(array, length - width, length, axis=dim)
        initial = lax.slice_in_dim(array, 0, width, axis=dim)
        before = lax.ppermute(last, axis, up)
        after = lax.ppermute(initial, axis, down)
        array = jnp.concatenate([before, array, after], axis=dim)
    return array


def broadcast(value, axis, source):
    kept = jnp.where(lax.axis_index(axis) == source, value, 0).astype(value.dtype)
    return lax.psum(kept, axis)


def stiffness(padded_field, padded_moduli, element_matrix):
    sources = padded_field.shape[1]
    span_x = padded_field.shape[2] - 1
    span_z = padded_field.shape[3] - 1
    span_y = padded_moduli.shape[2]
    corners = []
    for corner in range(8):
        along_x, along_z, along_y = (corner // 4, corner // 2 % 2, corner % 2)
        corners.append(
            padded_field[
                :,
                :,
                along_x : along_x + span_x,
                along_z : along_z + span_z,
                along_y : along_y + span_y,
            ]
        )
    stacked = jnp.stack(corners, 0).reshape(24, -1)
    forces = jnp.dot(
        element_matrix, stacked, precision=lax.Precision.HIGHEST, preferred_element_type=jnp.float32
    )
    forces = forces.reshape(8, 3, sources, span_x, span_z, span_y) * padded_moduli[1:, 1:, :]
    forces = jnp.pad(forces, ((0, 0), (0, 0), (0, 0), (0, 0), (0, 0), (0, 1)))
    summed = jnp.zeros((3, sources, span_x - 1, span_z - 1, span_y), jnp.float32)
    for corner in range(8):
        along_x, along_z, along_y = (corner // 4, corner // 2 % 2, corner % 2)
        summed = (
            summed
            + forces[
                corner,
                :,
                :,
                1 - along_x : 1 - along_x + span_x - 1,
                1 - along_z : 1 - along_z + span_z - 1,
                1 - along_y : 1 - along_y + span_y,
            ]
        )
    return summed


def pack_slots(values, targets, n_slab):
    node_count = values.shape[1]
    capacity = 2 * node_count // n_slab
    tile_owner = targets // PIX
    in_tile = targets % PIX
    onehot = (tile_owner[:, None] == jnp.arange(n_slab, dtype=jnp.int32)[None]).astype(jnp.int32)
    slot_rank = jnp.sum((jnp.cumsum(onehot, axis=0) - 1) * onehot, axis=1)
    send_vals = (
        jnp.zeros((values.shape[0], capacity, n_slab), jnp.float32)
        .at[:, slot_rank, tile_owner]
        .set(values)
    )
    send_ids = (
        jnp.zeros((1, capacity, n_slab), jnp.float32)
        .at[0, slot_rank, tile_owner]
        .set(in_tile.astype(jnp.float32))
    )
    return (send_vals, send_ids)


def bin_pixels(got_vals, got_ids):
    pixel_index = got_ids.reshape(-1).astype(jnp.int32)
    rows = got_vals.shape[0]
    return jnp.zeros((rows, PIX), jnp.float32).at[:, pixel_index].add(got_vals.reshape(rows, -1))


def body(
    right_side,
    smoother,
    material,
    moduli,
    element_matrix,
    coarse_inverse,
    surface_map,
    line_of_sight,
):
    components, sources, width_x, width_z, width_y = right_side.shape
    n_slab = lax.axis_size("slab")
    n_depth = lax.axis_size("depth")
    slab_rank = lax.axis_index("slab")
    depth_rank = lax.axis_index("depth")
    levels = jnp.arange(moduli.shape[0], dtype=jnp.int32)
    modulus_field = jnp.sum(
        jnp.where(material[None] == levels[:, None, None, None], moduli[:, None, None, None], 0.0),
        axis=0,
    )
    weights = smoother[:, None]
    agg_nodes = float(width_x * width_z * n_depth * width_y)
    block_sums = jnp.sum(right_side, axis=(2, 3, 4))
    placed = jnp.where(
        jnp.arange(n_slab, dtype=jnp.int32)[:, None, None] == slab_rank, block_sums[None], 0.0
    )
    placed = placed.reshape(components * n_slab, sources)
    coarse_sum = lax.psum(placed, ("slab", "depth"))
    coarse_vec = coarse_sum / agg_nodes
    correction = jnp.dot(
        coarse_inverse,
        coarse_vec,
        precision=lax.Precision.HIGHEST,
        preferred_element_type=jnp.float32,
    )
    by_block = correction.reshape(n_slab, components, sources)
    own_corr = lax.dynamic_index_in_dim(by_block, slab_rank, 0, keepdims=False)
    direction = weights * right_side + own_corr[:, :, None, None, None]
    numerator = lax.psum(jnp.sum(right_side * direction, axis=(0, 2, 3, 4)), ("slab", "depth"))
    stacked = jnp.concatenate(
        [direction.reshape(components * sources, width_x, width_z, width_y), modulus_field[None]], 0
    )
    halo_out = extended(stacked, (("slab", 1), ("depth", 2)), 1)
    padded = halo_out[: components * sources].reshape(
        components, sources, width_x + 2, width_z + 2, width_y
    )
    moduli_pad = halo_out[components * sources]
    padded = jnp.pad(padded, ((0, 0), (0, 0), (0, 0), (0, 0), (1, 0)))
    applied = stiffness(padded, moduli_pad, element_matrix)
    denominator = lax.psum(jnp.sum(direction * applied, axis=(0, 2, 3, 4)), ("slab", "depth"))
    step_size = numerator / denominator
    residual = right_side - step_size[None, :, None, None, None] * applied
    surface = step_size[None, :, None, None] * direction[:, :, :, width_z - 1, :]
    projected = jnp.sum(line_of_sight[:, None] * surface, axis=0).reshape(sources, -1)
    projected = broadcast(projected, "depth", n_depth - 1)
    targets = surface_map.reshape(-1)
    per_row = sources // n_depth
    send_vals, send_ids = pack_slots(projected, targets, n_slab)
    got_vals, got_ids = (
        lax.all_to_all(send_vals, "slab", split_axis=2, concat_axis=2, tiled=True),
        lax.all_to_all(send_ids, "slab", split_axis=2, concat_axis=2, tiled=True),
    )
    binned = bin_pixels(got_vals, got_ids)
    pixels = lax.dynamic_slice_in_dim(binned, depth_rank * per_row, per_row, 0)
    return (residual, pixels)


def solution(mesh):
    return jax.shard_map(
        body,
        mesh=mesh,
        in_specs=(
            P(None, None, "slab", "depth", None),
            P(None, "slab", "depth", None),
            P("slab", "depth", None),
            P(),
            P(),
            P(),
            P("slab", None),
            P(None, "slab", None),
        ),
        out_specs=(P(None, None, "slab", "depth", None), P("depth", "slab")),
        check_vma=False,
    )
```

profile of v0, /device:TPU:1, one launch (start us, length us, event | category | flops | bytes accessed | tf_op | source)
XLA Modules:
  0.0 356.4 jit_solution(3284111546868127449)
XLA Ops:
  0.8 0.2 broadcast_in_dim.78
  1.0 1.1 reduce_sum.56
  2.2 0.1 broadcast_select_fusion
  2.3 112.0 %psum.28 = f32[384,8]{1,0:T(8,128)S(1)} all-reduce(f32[384,8]{1,0:T(8,128)S(1)} %broadcast_select_fusion), channel_id=1, replica_groups=mesh['slab'=128,'depth'=4] {'slab','depth'}, use_global_device_ids=true, to_apply=%region_1.2 | all-reduce | flops 3072 | bytes 24576 | tf_op jit(solution)/shard_map/psum | solution.py:120
  114.3 0.7 convolution_bitcast_fusion.1
  115.0 0.2 copy.73
  115.3 0.8 select_reduce_fusion
  116.1 1.0 fusion.23
  117.2 2.7 collective-permute-start.1
  119.9 2.8 collective-permute-start
  122.8 0.1 copy.78
  122.9 0.2 fusion.25
  123.2 0.2 fusion.26
  123.5 11.4 %scatter_fusion = f32[4,128]{1,0:T(4,128)S(1)} fusion(f32[4,128]{1,0:T(4,128)S(1)} %broadcast.273, s32[256]{0:T(256)S(1)} %bitcast.126, f32[256]{0:T(256)S(1)} %get-tuple-element.21), kind=kCustom, calls=%fused_computation | custom fusion | bytes 5120 | tf_op jit(solution)/shard_map/scatter | solution.py:82
  134.9 0.7 copy.80
  135.7 10.0 %all-to-all-start = ((f32[1,4,128]{1,0,2:T(1,128)}), f32[1,4,128]{1,0,2:T(1,128)S(1)}, u32[]{:S(2)}, u32[]{:S(2)}) async-start(f32[1,4,128]{1,0,2:T(1,128)} %copy.80), calls=%async_computation | async-start | bytes 131072 | tf_op jit(solution)/shard_map/all_to_all | solution.py:153
  145.6 14.9 %all-to-all-done = f32[1,4,128]{1,0,2:T(1,128)S(1)} async-done(((f32[1,4,128]{1,0,2:T(1,128)}), f32[1,4,128]{1,0,2:T(1,128)S(1)}, u32[]{:S(2)}, u32[]{:S(2)}) %all-to-all-start) | async-done | bytes 2080 | tf_op jit(solution)/shard_map/all_to_all | solution.py:153
  160.7 0.1 pad_maximum_fusion.5
  160.8 2.3 collective-permute-start.2
  163.1 1.5 collective-permute-start.3
  164.6 3.6 %collective-permute-done.3 = f32[25,3,1,256]{3,2,0,1:T(1,128)S(1)} collective-permute-done((f32[25,3,1,256]{3,2,0,1:T(1,128)S(1)}, f32[25,3,1,256]{3,2,0,1:T(1,128)S(1)}, u32[]{:S(2)}, u32[]{:S(2)}) %collective-permute-start.3) | collective-permute-done | bytes 76832 | tf_op jit(solution)/shard_map/ppermute | solution.py:17
  168.2 0.2 pad_maximum_fusion
  168.5 0.1 slice.111
  168.7 1.1 fusion.1
  169.8 1.0 fusion.11
  170.8 1.2 fusion.3
  172.0 1.0 fusion.10
  173.0 1.1 fusion.5
  174.1 1.0 fusion.9
  175.1 1.2 fusion.7
  176.3 1.0 fusion.8
  177.3 5.7 %reshape.373 = f32[24,36864]{1,0:T(8,128)} reshape(f32[8,3,8,2,9,256]{5,4,3,2,1,0:T(8,128)} %fusion.8) | data formatting | bytes 7077888 | tf_op jit(solution)/shard_map/reshape | solution.py:44
  183.0 6.9 %convolution_bitcast_fusion = f32[24,36864]{1,0:T(8,128)} fusion(f32[24,36864]{1,0:T(8,128)} %reshape.373, f32[24,24]{1,0:T(8,128)S(1)} %copy-done.3), kind=kOutput, calls=%fused_computation.3 | convolution fusion | flops 254803968 | bytes 7080192 | tf_op jit(solution)/shard_map/dot_general | solution.py:45
  189.9 5.3 %reshape.374 = f32[8,3,8,2,9,256]{5,4,3,2,1,0:T(8,128)} reshape(f32[24,36864]{1,0:T(8,128)} %convolution_bitcast_fusion) | data formatting | bytes 7077888 | tf_op jit(solution)/shard_map/reshape | solution.py:48
  195.2 3.6 %broadcast_multiply_fusion = f32[8,3,8,2,9,256]{5,4,3,2,1,0:T(8,128)S(1)} fusion(f32[8,3,8,2,9,256]{5,4,3,2,1,0:T(8,128)} %reshape.374, f32[2,9,256]{2,1,0:T(8,128)S(1)} %slice.116), kind=kLoop, calls=%fused_computation.8 | loop fusion | flops 884736 | bytes 7096320 | tf_op jit(solution)/shard_map/mul | solution.py:48
  198.8 0.4 fusion.19
  199.2 99.5 %all-reduce.2 = (f32[8]{0:T(128)S(1)}, f32[8]{0:T(128)S(1)}) all-reduce(f32[8]{0:T(128)S(1)} %get-tuple-element.15, f32[8]{0:T(128)S(1)} %get-tuple-element.14), channel_id=1, replica_groups=mesh['slab'=128,'depth'=4] {'slab','depth'}, use_global_device_ids=true, to_apply=%region_3.4 | all-reduce | flops 16 | bytes 128 | tf_op jit(solution)/shard_map/psum | solution.py:131
  298.7 0.1 fusion.34
  298.8 8.5 %psum.31 = f32[8,256]{1,0:T(8,128)S(1)} all-reduce(f32[8,256]{1,0:T(8,128)S(1)} %broadcast_select_fusion.1), channel_id=1, replica_groups=mesh['slab'=128,'depth'=4] {'depth'}, use_global_device_ids=true, to_apply=%region_12.13 | all-reduce | flops 2048 | bytes 16384 | tf_op jit(solution)/shard_map/psum | solution.py:24
  307.3 0.1 copy.82
  307.5 12.1 %scatter_fusion.1 = f32[8,4,128]{0,2,1:T(8,128)S(1)} fusion(f32[8,4,128]{0,2,1:T(8,128)S(1)} %broadcast_in_dim.91, s32[256]{0:T(256)S(1)} %bitcast.127, f32[256,8]{1,0:T(8,128)S(1)} %copy.82), kind=kCustom, calls=%fused_computation.1 | custom fusion | bytes 26624 | tf_op jit(solution)/shard_map/scatter | solution.py:77
  319.6 0.9 copy.83
  320.4 9.6 %all-to-all-start.1 = ((f32[8,4,128]{0,1,2:T(4,128)}), f32[8,4,128]{0,1,2:T(4,128)S(1)}, u32[]{:S(2)}, u32[]{:S(2)}) async-start(f32[8,4,128]{0,1,2:T(4,128)} %copy.83), calls=%async_computation.1 | async-start | bytes 524288 | tf_op jit(solution)/shard_map/all_to_all | solution.py:152
  330.0 0.8 fusion.21
  330.8 21.7 %all-to-all-done.1 = f32[8,4,128]{0,1,2:T(4,128)S(1)} async-done(((f32[8,4,128]{0,1,2:T(4,128)}), f32[8,4,128]{0,1,2:T(4,128)S(1)}, u32[]{:S(2)}, u32[]{:S(2)}) %all-to-all-start.1) | async-done | bytes 16416 | tf_op jit(solution)/shard_map/all_to_all | solution.py:152
  352.6 0.2 copy.86
  352.8 2.8 scatter_custom_fusion.2
  355.7 0.7 copy.88
  (43 shorter events, 0.9 us)
Async XLA Ops:
  0.6 113.7 %copy-start = (f32[384,384]{1,0:T(8,128)S(1)}, f32[384,384]{1,0:T(8,128)}, u32[]{:S(2)}) copy-start(f32[384,384]{1,0:T(8,128)} %param.13) | copy-start | bytes 1769476
  0.6 122.1 %copy-start.4 = (s32[1,256]{1,0:T(1,128)S(1)}, s32[1,256]{1,0:T(1,128)}, u32[]{:S(2)}) copy-start(s32[1,256]{1,0:T(1,128)} %param.14) | copy-start | bytes 3076
  2.1 143.5 %copy-start.5 = (f32[3,1,256]{2,1,0:T(1,128)S(1)}, f32[3,1,256]{2,1,0:T(1,128)}, u32[]{:S(2)}) copy-start(f32[3,1,256]{2,1,0:T(1,128)} %param.15) | copy-start | bytes 9220
  117.2 43.5 %collective-permute-start.1 = (f32[25,1,8,256]{3,2,0,1:T(8,128)S(1)}, f32[25,1,8,256]{3,2,0,1:T(8,128)S(1)}, u32[]{:S(2)}, u32[]{:S(2)}) collective-permute-start(f32[25,1,8,256]{3,2,0,1:T(8,128)S(1)} %pad_maximum_fusion.1), channel_id=1, source_target_pairs={{4,0},{8,4},{12,8},{16,12},{20,16},{24,20},{28,24},{32,28},{36,32}... | collective-permute-start | bytes 614408 | tf_op jit(solution)/shard_map/ppermute | solution.py:17
  119.9 40.8 %collective-permute-start = (f32[25,1,8,256]{3,2,0,1:T(8,128)S(1)}, f32[25,1,8,256]{3,2,0,1:T(8,128)S(1)}, u32[]{:S(2)}, u32[]{:S(2)}) collective-permute-start(f32[25,1,8,256]{3,2,0,1:T(8,128)S(1)} %pad_maximum_fusion.1), channel_id=1, source_target_pairs={{0,4},{4,8},{8,12},{12,16},{16,20},{20,24},{24,28},{28,32},{32,36}... | collective-permute-start | bytes 614408 | tf_op jit(solution)/shard_map/ppermute | solution.py:16
  135.7 24.9 %all-to-all-start = ((f32[1,4,128]{1,0,2:T(1,128)}), f32[1,4,128]{1,0,2:T(1,128)S(1)}, u32[]{:S(2)}, u32[]{:S(2)}) async-start(f32[1,4,128]{1,0,2:T(1,128)} %copy.80), calls=%async_computation | async-start | bytes 131072 | tf_op jit(solution)/shard_map/all_to_all | solution.py:153
  160.8 3.8 %collective-permute-start.2 = (f32[25,3,1,256]{3,2,0,1:T(1,128)S(1)}, f32[25,3,1,256]{3,2,0,1:T(1,128)S(1)}, u32[]{:S(2)}, u32[]{:S(2)}) collective-permute-start(f32[25,3,1,256]{3,2,0,1:T(1,128)S(1)} %get-tuple-element.19), channel_id=1, source_target_pairs={{0,1},{1,2},{2,3},{4,5},{5,6},{6,7},{8,9},{9,10},{10,11},{12,13},{... | collective-permute-start | bytes 230408 | tf_op jit(solution)/shard_map/ppermute | solution.py:16
  163.1 5.1 %collective-permute-start.3 = (f32[25,3,1,256]{3,2,0,1:T(1,128)S(1)}, f32[25,3,1,256]{3,2,0,1:T(1,128)S(1)}, u32[]{:S(2)}, u32[]{:S(2)}) collective-permute-start(f32[25,3,1,256]{3,2,0,1:T(1,128)S(1)} %get-tuple-element.20), channel_id=1, source_target_pairs={{1,0},{2,1},{3,2},{5,4},{6,5},{7,6},{9,8},{10,9},{11,10},{13,12},{... | collective-permute-start | bytes 230408 | tf_op jit(solution)/shard_map/ppermute | solution.py:17
  177.3 5.7 %copy-start.3 = (f32[24,24]{1,0:T(8,128)S(1)}, f32[24,24]{1,0:T(8,128)}, u32[]{:S(2)}) copy-start(f32[24,24]{1,0:T(8,128)} %param.12) | copy-start | bytes 6916
  195.2 3.6 %copy-start.1 = (f32[3,8,1,8,256]{4,3,2,1,0:T(8,128)S(1)}, f32[3,8,1,8,256]{4,3,2,1,0:T(8,128)}, u32[]{:S(2)}) copy-start(f32[3,8,1,8,256]{4,3,2,1,0:T(8,128)} %param.8) | copy-start | bytes 589828
  195.2 3.7 %copy-start.2 = (f32[3,1,8,256]{3,2,1,0:T(8,128)S(1)}, f32[3,1,8,256]{3,2,1,0:T(8,128)}, u32[]{:S(2)}) copy-start(f32[3,1,8,256]{3,2,1,0:T(8,128)} %param.9) | copy-start | bytes 73732
  320.4 32.1 %all-to-all-start.1 = ((f32[8,4,128]{0,1,2:T(4,128)}), f32[8,4,128]{0,1,2:T(4,128)S(1)}, u32[]{:S(2)}, u32[]{:S(2)}) async-start(f32[8,4,128]{0,1,2:T(4,128)} %copy.83), calls=%async_computation.1 | async-start | bytes 524288 | tf_op jit(solution)/shard_map/all_to_all | solution.py:152
where the time goes:
time: 357 us; the launch traced here: 356 us
  blocking collectives  220 us (62%)
  local copies, waits for them, and re-layouts  47 us (13%)
  waiting for transfers between devices  40.3 us (11%)
  starting transfers between devices  28.8 us (8%)
  other arithmetic  11.7 us (3%)
  matrix products  7.56 us (2%)
    psum x1, blocking collectives, body(): coarse_sum = lax.psum(placed, ('slab', 'depth'))  112 us
    psum x1, blocking collectives, body(): lax.psum(jnp.sum(right_side * direction, axis=(0, 2, 3, 4)), ('slab', 'de...  99.5 us
    all_to_all x1, waiting for transfers between devices, body(): lax.all_to_all(send_vals, 'slab', split_axis=2, concat_axis=2, tiled=True)  21.7 us
    all_to_all x1, waiting for transfers between devices, body(): lax.all_to_all(send_ids, 'slab', split_axis=2, concat_axis=2, tiled=True)  14.9 us
    scatter x2, local copies, waits for them, and re-layouts, pack_slots(): send_vals = jnp.zeros((values.shape[0], capacity, n_slab), jnp.float32).a...  12.9 us
    scatter x2, local copies, waits for them, and re-layouts, pack_slots(): send_ids = jnp.zeros((1, capacity, n_slab), jnp.float32).at[0, slot_rank,...  12.2 us
    all_to_all x1, starting transfers between devices, body(): lax.all_to_all(send_ids, 'slab', split_axis=2, concat_axis=2, tiled=True)  9.95 us
    all_to_all x1, starting transfers between devices, body(): lax.all_to_all(send_vals, 'slab', split_axis=2, concat_axis=2, tiled=True)  9.59 us
  transfers between devices with their start and end apart: 6, of which 3 were waited for; matrix products, arithmetic and copies ran while one was open for 4% of the time, Pallas kernels for 0%

commit v1 on v0

v1 whole, which is shorter than its diff:
```python
import jax
import jax.numpy as jnp
from jax import lax
from jax.experimental import pallas as pl
from jax.experimental.pallas import tpu as pltpu
from jax.sharding import PartitionSpec as P

F32, BF16 = jnp.float32, jnp.bfloat16
MESH = pl.DeviceIdType.MESH
HIGHEST = lax.Precision.HIGHEST
NX, NZ, NC, ND = 4, 16, 2, 4
SLABS, ROWS, NY = NX * NZ * NC, 8, 256
NODES = ROWS * ND * NY


def iota(shape, dim):
    return lax.broadcasted_iota(jnp.int32, shape, dim)


def dot(a, b):
    return jnp.dot(a, b, preferred_element_type=F32)


def dot_full(a, b):
    return jnp.dot(a, b, preferred_element_type=F32, precision=HIGHEST)


def dot_nt(a, b):
    return lax.dot_general(a, b, (((1,), (1,)), ((), ())), preferred_element_type=F32)


def split(v):
    high = v.astype(BF16)
    return high, (v - high.astype(F32)).astype(BF16)


def fsplit(v):
    high = v.astype(BF16).astype(F32)
    return high, v - high


def hot(mask):
    return jnp.where(mask, 1.0, 0.0).astype(F32)


def from_right(v):
    width = v.shape[1]
    return jnp.where(iota(v.shape, 1) == width - 1, 0.0, pltpu.roll(v, width - 1, axis=1))


def from_left(v):
    return jnp.where(iota(v.shape, 1) == 0, 0.0, pltpu.roll(v, 1, axis=1))


def to_row(columns):
    lane, sub = iota((8, 128), 1), iota((8, 128), 0)
    total = jnp.zeros((8, 128), F32)
    for q, column in enumerate(columns):
        total = jnp.where(lane == q * 8 + sub, column, total)
    return jnp.sum(total, axis=0, keepdims=True)


def pick_row(v, index):
    return jnp.sum(jnp.where(iota(v.shape, 0) == index, v, 0.0), axis=0, keepdims=True)


def kernel(
    r_ref, s_ref, mat_ref, mod_ref, e_ref, c_ref, map_ref, los_ref,
    res_ref, pix_ref,
    rt, st, hp, hz, own_mod, mod_in, mods, w, f_own, lhs_own, lhs_nb, app, g_z,
    c_perm, pj_out, pj_in, y_out, y_in, ms, r1, r2, gps,
    ly_out, ly_in, lz_out, lz_in, lx_out, lx_in,
    send, recv,
):
    s, d = lax.axis_index("slab"), lax.axis_index("depth")
    x, z, c = s // 32, (s // 2) % 16, s % 2
    g = x * 2 + c
    up, down = lax.rem(s + 1, SLABS), lax.rem(s + SLABS - 1, SLABS)
    deeper, higher = lax.rem(d + 1, ND), lax.rem(d + ND - 1, ND)

    y_peers = [(s, lax.rem(d + i, ND)) for i in range(1, ND)]
    z_ids = [lax.rem(z + i, NZ) for i in range(1, NZ)]
    z_peers = [(x * 32 + i * 2 + c, d) for i in z_ids]
    g_ids = [lax.rem(g + i, 8) for i in range(1, 8)]
    g_peers = [((i // 2) * 32 + z * 2 + i % 2, d) for i in g_ids]
    near = [(up, d), (down, d)] + [(a, b) for a in (up, down) for b in (deeper, higher)]

    barrier = pltpu.get_barrier_semaphore()
    peers = y_peers + z_peers + g_peers + near
    for peer in peers:
        pl.semaphore_signal(barrier, inc=1, device_id=peer, device_id_type=MESH)

    def copy(src, dst, index, peer):
        return pltpu.make_async_remote_copy(
            src_ref=src, dst_ref=dst, send_sem=send.at[index], recv_sem=recv.at[index],
            device_id=peer, device_id_type=MESH,
        )

    field = jnp.transpose(r_ref[...], (1, 0, 2))
    rt[...] = field
    for k in range(ROWS):
        weight = jnp.concatenate(
            [jnp.broadcast_to(s_ref[m, k : k + 1, :], (8, NY)) for m in range(3)], axis=0
        )
        st[k] = field[k] * weight
    material = mat_ref[...]
    modulus = jnp.zeros((ROWS, NY), F32)
    for i in range(16):
        modulus = jnp.where(material == i, mod_ref[i], modulus)
    own_mod[...] = modulus
    sums = jnp.sum(jnp.sum(field, axis=0), axis=1, keepdims=True)
    blocks = [sums[m * 8 : m * 8 + 8] for m in range(3)]
    row = to_row(blocks)
    y_out[...] = row
    y_in[d] = row
    shown = jnp.zeros((8, NY), F32)
    for m in range(3):
        shown = shown + los_ref[m] * st[ROWS - 1, m * 8 : m * 8 + 8, :]
    pj_out[...] = shown

    pl.semaphore_wait(barrier, len(peers))

    started = []
    for i, peer in enumerate(y_peers):
        started.append(copy(y_out, y_in.at[d], i, peer))
        started[-1].start()
    for i, peer in enumerate([(down, d), (s, higher), (down, higher)]):
        started.append(copy(own_mod, mod_in.at[i], 3 + i, peer))
        started[-1].start()

    def shows():
        return [copy(pj_out, pj_in, 6 + i, (s, i)) for i in range(ND - 1)]

    @pl.when(d == ND - 1)
    def _():
        for each in shows():
            each.start()
        pj_in[...] = shown

    sides = []
    for plane, a in ((1, s), (2, down), (0, up)):
        sides.append((st.at[0], hz.at[plane, 1], (a, higher)))
        sides.append((st.at[ROWS - 1], hz.at[plane, 0], (a, deeper)))
    for i, (src, dst, peer) in enumerate(sides):
        started.append(copy(src, dst, 9 + i, peer))
        started[-1].start()
    for i, (plane, peer) in enumerate(((1, (down, d)), (0, (up, d)))):
        started.append(copy(st, hp.at[plane], 15 + i, peer))
        started[-1].start()

    target = map_ref[...]
    tile, in_tile = target >> 8, target & 255
    tile_col = jnp.transpose(jnp.broadcast_to(tile.astype(F32), (8, NY)))[:, 0:1]
    same = (tile_col == tile.astype(F32)) & (iota((NY, NY), 0) < iota((NY, NY), 1))
    rank = jnp.sum(hot(same), axis=0, keepdims=True).astype(jnp.int32)
    tile_g = (tile >> 5) * 2 + (tile & 1)
    place_row = (tile_g >> 2) * 16 + ((tile >> 1) & 15)
    place_lane = (tile_g & 3) * 32 + rank
    row_hot = hot(iota((32, NY), 0) == place_row)

    e = e_ref[...]
    rho, eps = iota((192, 24), 0), iota((192, 24), 1)
    picked = dot_full(hot(eps == (rho % 96) // 8 + 12 * (1 - rho // 96)), e)
    eps, kap = iota((24, 192), 0), iota((24, 192), 1)
    column = 6 * (kap // 96) + (kap % 48) // 8
    wide = [dot_full(picked, hot(eps == column + 12 * a)) for a in range(2)]
    rho, kap = iota((96, 192), 0), iota((96, 192), 1)
    same_source = rho % 8 == kap % 8
    first = same_source & (kap % 96 < 48)
    parts = [wide[1][:96], wide[0][96:], wide[0][:96], wide[1][96:]]
    for i, part in enumerate(parts):
        high, low = fsplit(part)
        high = jnp.where(same_source, high, 0.0).astype(BF16)
        low = jnp.where(first, low, 0.0).astype(BF16)
        if i < 2:
            lhs_own[0, i * 96 : i * 96 + 96] = high
            lhs_own[1, i * 96 : i * 96 + 96] = low
        else:
            lhs_nb[i - 2, 0] = high
            lhs_nb[i - 2, 1] = low

    @pl.when(d != ND - 1)
    def _():
        copy(pj_out, pj_in, 6 + d, (s, d)).wait_recv()

    for i in range(3):
        copy(y_out, y_in.at[0], i, y_peers[i]).wait_recv()
    block_row = y_in[0] + y_in[1] + y_in[2] + y_in[3]
    shown = pj_in[...]
    values = [pick_row(shown, 2 * d), pick_row(shown, 2 * d + 1)]
    values += [los_ref[m] for m in range(3)] + [in_tile.astype(F32)]
    packed = jnp.zeros((64, 128), F32)
    for v, value in enumerate(values):
        high, low = fsplit(value)
        left = jnp.concatenate([row_hot * high, row_hot * low], axis=0).astype(BF16)
        right = hot(iota((128, NY), 0) == place_lane + 4 * v).astype(BF16)
        packed = packed + dot_nt(left, right)
    packed = packed[:32] + packed[32:]
    ms[:, 0] = packed[:16].reshape(16, 1, 128)
    ms[:, 1] = jnp.broadcast_to(block_row.reshape(1, 1, 128), (16, 1, 128))
    ms[:, 2] = packed[16:].reshape(16, 1, 128)
    r1[z] = ms[z]
    for i, peer in enumerate(z_peers):
        started.append(copy(ms.at[z_ids[i]], r1.at[z], 17 + i, peer))
        started[-1].start()

    def weave(plane, index, value, alive):
        if alive is not None:
            value = jnp.where(alive, value, 0.0)
        high, low = split(jnp.concatenate([from_left(value), value], axis=0))
        w[plane, index * 96 : index * 96 + 48] = high
        w[plane, index * 96 + 48 : index * 96 + 96] = low

    for k in range(ROWS):
        weave(1, k + 1, st[k], None)

    order = hot(iota((384, 384), 0) == 3 * (iota((384, 384), 1) % 128) + iota((384, 384), 1) // 128)
    order_t = hot(iota((384, 384), 1) == 3 * (iota((384, 384), 0) % 128) + iota((384, 384), 0) // 128)
    order, order_t = order.astype(BF16), order_t.astype(BF16)
    for i, part in enumerate(split(c_ref[...])):
        c_perm[i] = dot(order_t, dot(part, order).astype(BF16)).astype(BF16)

    for i in range(3):
        copy(own_mod, mod_in.at[i], 3 + i, (down, d)).wait_recv()
    inner = d < ND - 1
    last = s == SLABS - 1
    for k in range(ROWS):
        mods[0, k] = own_mod[k : k + 1, :]
        mods[1, k] = jnp.where(last, 0.0, mod_in[0, k : k + 1, :])
    mods[0, ROWS] = jnp.where(inner, mod_in[1, 0:1, :], 0.0)
    mods[1, ROWS] = jnp.where(inner & jnp.logical_not(last), mod_in[2, 0:1, :], 0.0)

    for i in range(6):
        copy(st.at[0], hz.at[0, 0], 9 + i, (s, higher)).wait_recv()
    not_first, not_last = s > 0, s < SLABS - 1
    weave(1, 0, hz[1, 0], d > 0)
    weave(1, 9, hz[1, 1], inner)

    for i in range(15):
        copy(ms.at[0], r1.at[0], 17 + i, (down, d)).wait_recv()
    for i, peer in enumerate(g_peers):
        half = g_ids[i] // 4
        started.append(copy(r1.at[:, pl.ds(half, 2)], r2.at[x, :, c], 32 + i, peer))
        started[-1].start()
    half = g // 4
    for k in range(NZ):
        r2[x, k, c] = r1[k, pl.ds(half, 2)]

    for k in range(ROWS + 1):
        block = w[1, 96 * k : 96 * k + 192]
        f = dot(lhs_own[0], block) + dot(lhs_own[1], block)
        f_own[k] = mods[0, k] * f[:96] + mods[1, k] * f[96:]

    rho, eps = iota((128, 24), 0), iota((128, 24), 1)
    corner, rest = rho // 32, rho % 32
    comp, plane, comp2 = rest // 9, (rest % 9) // 3, rest % 3
    left = jnp.zeros((128, 8), F32)
    for layer in range(2):
        rows = dot_full(hot((eps == 12 * (1 - layer) + 3 * corner + comp) & (rest < 27)), e)
        keep = (eps % 3 == comp2) & (eps // 12 == plane - layer)
        of, to = iota((24, 8), 0), iota((24, 8), 1)
        gather = hot((to // 4 == layer) & ((of % 12) // 3 == to % 4))
        left = left + dot_full(jnp.where(keep, rows, 0.0), gather)
    high, low = fsplit(left)
    left_high = jnp.concatenate([high, high], axis=1).astype(BF16)
    left_low = jnp.concatenate([low, jnp.zeros_like(low)], axis=1).astype(BF16)
    before = None
    for k in range(ROWS + 1):
        sub, lane = iota((8, NY), 0), iota((8, NY), 1)
        block = jnp.where(sub < 4, mods[0, k], mods[1, k])
        there = (sub % 2 == 1) | (lane > 0)
        if k == 0:
            there = there & ((sub % 4 >= 2) | (d > 0))
        block = jnp.where(there, block, 0.0)
        high, low = fsplit(block)
        block = jnp.concatenate([high, low], axis=0).astype(BF16)
        now = dot(left_high, block) + dot(left_low, block)
        if before is not None:
            both = before[64:] + now[:64]
            g_z[k - 1] = both[32:] + from_right(both[:32])
        before = now

    for i in range(2):
        copy(st, hp.at[i], 15 + i, (down, d)).wait_recv()
    for plane, index, alive in ((0, 0, not_first), (2, 1, not_last)):
        weave(plane, 0, hz[plane, 0], alive & (d > 0))
        weave(plane, 9, hz[plane, 1], alive & inner)
        for k in range(ROWS):
            weave(plane, k + 1, hp[index, k], alive)
    before = None
    for k in range(ROWS + 1):
        now = f_own[k]
        for i in range(2):
            block = w[2 * i, 96 * k : 96 * k + 192]
            now = now + mods[i, k] * (dot(lhs_nb[i, 0], block) + dot(lhs_nb[i, 1], block))
        if before is not None:
            both = before[48:] + now[:48]
            app[k - 1] = both[24:] + from_right(both[:24])
        before = now

    for i in range(7):
        copy(r1.at[:, pl.ds(0, 2)], r2.at[0, :, 0], 32 + i, (down, d)).wait_recv()
    flat = r2.reshape(2 * SLABS, 128)
    means = jnp.transpose(flat[pl.ds(1 - half, SLABS, stride=2), :]) * (1.0 / NODES)
    gps[...] = jnp.transpose(flat[pl.ds(half, SLABS, stride=2), :])
    means = jnp.concatenate([means[m * 8 : m * 8 + 8] for m in range(3)], axis=1)
    high, low = fsplit(means)
    both = jnp.concatenate([high, low], axis=0).astype(BF16)
    solved = dot(both, c_perm[0])
    corr = solved[:8] + solved[8:] + dot(both, c_perm[1])[:8]
    lane = iota((8, 128), 1)
    mine = [
        [
            jnp.sum(
                jnp.where(lane == s + p - 1, corr[:, m * 128 : m * 128 + 128], 0.0),
                axis=1,
                keepdims=True,
            )
            for m in range(3)
        ]
        for p in range(3)
    ]
    own = jnp.concatenate(mine[1], axis=0)
    near_sum = jnp.zeros((24, NY), F32)
    force_sum = jnp.zeros((24, NY), F32)
    for k in range(ROWS):
        grown = []
        for m in range(3):
            total = app[k, m * 8 : m * 8 + 8]
            for p in range(3):
                for m2 in range(3):
                    i = m * 9 + p * 3 + m2
                    total = total + mine[p][m2] * g_z[k, i : i + 1]
            grown.append(total)
        total = jnp.concatenate(grown, axis=0)
        app[k] = total
        direction = st[k] + own
        near_sum = near_sum + direction * total
        force_sum = force_sum + direction * rt[k]
    near_sum = jnp.sum(near_sum, axis=1, keepdims=True)
    force_sum = jnp.sum(force_sum, axis=1, keepdims=True)
    row = to_row(
        [
            force_sum[:8] + force_sum[8:16] + force_sum[16:],
            near_sum[:8] + near_sum[8:16] + near_sum[16:],
        ]
    )

    ly_out[...] = row
    ly_in[d] = row
    for i, peer in enumerate(y_peers):
        started.append(copy(ly_out, ly_in.at[d], 39 + i, peer))
        started[-1].start()

    group = gps[pl.ds(pl.multiple_of((g % 4) * 32, 32), 32), :]
    found = []
    for v in range(2):
        value = group[4 * v : 4 * v + 4]
        for m in range(3):
            value = value + group[8 + 4 * m : 12 + 4 * m] * pick_row(
                corr[:, m * 128 : m * 128 + 128], 2 * d + v
            )
        found.append(jnp.concatenate([value[j : j + 1] for j in range(4)], axis=1))
    ids = group[20:24].astype(jnp.int32)
    sub = iota((8, 512), 0)
    parts = [fsplit(v) for v in found]
    left = jnp.where(sub == 0, parts[0][0], jnp.where(sub == 1, parts[1][0], 0.0))
    left = jnp.where(sub == 2, parts[0][1], jnp.where(sub == 3, parts[1][1], left))
    right = jnp.concatenate([hot(iota((256, 128), 0) == ids[j : j + 1]) for j in range(4)], axis=1)
    bins = dot_nt(left.astype(BF16), right.astype(BF16))

    for i in range(3):
        copy(ly_out, ly_in.at[0], 39 + i, y_peers[i]).wait_recv()
    row = ly_in[0] + ly_in[1] + ly_in[2] + ly_in[3]
    lz_out[...] = row
    lz_in[z] = row
    for i, peer in enumerate(z_peers):
        started.append(copy(lz_out, lz_in.at[z], 42 + i, peer))
        started[-1].start()
    for i in range(15):
        copy(lz_out, lz_in.at[0], 42 + i, (down, d)).wait_recv()
    row = jnp.sum(lz_in[...], axis=0)
    lx_out[...] = row
    lx_in[g] = row
    for i, peer in enumerate(g_peers):
        started.append(copy(lx_out, lx_in.at[g], 57 + i, peer))
        started[-1].start()
    for i in range(7):
        copy(lx_out, lx_in.at[0], 57 + i, (down, d)).wait_recv()
    row = jnp.broadcast_to(jnp.sum(lx_in[...], axis=0), (8, 128))
    lane, sub = iota((8, 128), 1), iota((8, 128), 0)
    numerator = jnp.sum(jnp.where(lane == sub, row, 0.0), axis=1, keepdims=True)
    denominator = jnp.sum(jnp.where(lane == sub + 8, row, 0.0), axis=1, keepdims=True)
    step = numerator / denominator
    steps = jnp.concatenate([step] * 3, axis=0)
    res_ref[...] = jnp.transpose(rt[...] - steps * app[...], (1, 0, 2))
    wide_step = jnp.broadcast_to(step, (8, NY))
    for v in range(2):
        pix_ref[v : v + 1, :] = pick_row(wide_step, 2 * d + v) * (
            bins[v : v + 1] + bins[v + 2 : v + 3]
        )

    for each in started:
        each.wait_send()

    @pl.when(d == ND - 1)
    def _():
        for each in shows():
            each.wait_send()


def body(right_side, smoother, material, moduli, element_matrix, coarse_inverse, surface_map, line_of_sight):
    vmem = pl.BlockSpec(memory_space=pltpu.VMEM)
    smem = pl.BlockSpec(memory_space=pltpu.SMEM)
    residual, pixels = pl.pallas_call(
        kernel,
        out_shape=(
            jax.ShapeDtypeStruct((24, ROWS, NY), F32),
            jax.ShapeDtypeStruct((2, NY), F32),
        ),
        in_specs=[vmem, vmem, vmem, smem, vmem, vmem, vmem, vmem],
        out_specs=(vmem, vmem),
        scratch_shapes=[
            pltpu.VMEM((ROWS, 24, NY), F32),
            pltpu.VMEM((ROWS, 24, NY), F32),
            pltpu.VMEM((2, ROWS, 24, NY), F32),
            pltpu.VMEM((3, 2, 24, NY), F32),
            pltpu.VMEM((ROWS, NY), F32),
            pltpu.VMEM((3, ROWS, NY), F32),
            pltpu.VMEM((2, ROWS + 1, 1, NY), F32),
            pltpu.VMEM((3, 960, NY), BF16),
            pltpu.VMEM((ROWS + 1, 96, NY), F32),
            pltpu.VMEM((2, 192, 192), BF16),
            pltpu.VMEM((2, 2, 96, 192), BF16),
            pltpu.VMEM((ROWS, 24, NY), F32),
            pltpu.VMEM((ROWS, 32, NY), F32),
            pltpu.VMEM((2, 384, 384), BF16),
            pltpu.VMEM((8, NY), F32),
            pltpu.VMEM((8, NY), F32),
            pltpu.VMEM((1, 128), F32),
            pltpu.VMEM((ND, 1, 128), F32),
            pltpu.VMEM((NZ, 3, 1, 128), F32),
            pltpu.VMEM((NZ, 3, 1, 128), F32),
            pltpu.VMEM((NX, NZ, NC, 2, 1, 128), F32),
            pltpu.VMEM((128, 128), F32),
            pltpu.VMEM((1, 128), F32),
            pltpu.VMEM((ND, 1, 128), F32),
            pltpu.VMEM((1, 128), F32),
            pltpu.VMEM((NZ, 1, 128), F32),
            pltpu.VMEM((1, 128), F32),
            pltpu.VMEM((8, 1, 128), F32),
            pltpu.SemaphoreType.DMA((64,)),
            pltpu.SemaphoreType.DMA((64,)),
        ],
        compiler_params=pltpu.CompilerParams(
            collective_id=0, has_side_effects=True, vmem_limit_bytes=40 * 1024 * 1024
        ),
    )(
        right_side.reshape(24, ROWS, NY),
        smoother.reshape(3, ROWS, NY),
        material.reshape(ROWS, NY),
        moduli,
        element_matrix,
        coarse_inverse,
        surface_map,
        line_of_sight,
    )
    return residual.reshape(right_side.shape), pixels


def solution(mesh):
    return jax.shard_map(
        body,
        mesh=mesh,
        in_specs=(
            P(None, None, "slab", "depth", None),
            P(None, "slab", "depth", None),
            P("slab", "depth", None),
            P(),
            P(),
            P(),
            P("slab", None),
            P(None, "slab", None),
        ),
        out_specs=(P(None, None, "slab", "depth", None), P("depth", "slab")),
        check_vma=False,
    )
```

time: 357 us -> 55.6 us (0.16)
  blocking collectives: 220 us -> 0 us
  Pallas kernels: 0 us -> 48.5 us
  local copies, waits for them, and re-layouts: 47 us -> 6.06 us
  waiting for transfers between devices: 40.3 us -> 0 us
  starting transfers between devices: 28.8 us -> 0 us
  other arithmetic: 11.7 us -> 0 us
  matrix products: 7.56 us -> 0 us
    psum x3 -> x0, blocking collectives: 220 us -> none  [the longest x1 112 us: body(): coarse_sum = lax.psum(placed, ('slab', 'depth'))]
    pallas_call x0 -> x1, Pallas kernels: none -> 48.5 us  [body(): pl.pallas_call(kernel, out_shape=(jax.ShapeDtypeStruct((24, ROWS, NY), F3...]
    all_to_all x2 -> x0, waiting for transfers between devices: 36.7 us -> none  [the longest x1 21.7 us: body(): lax.all_to_all(send_vals, 'slab', split_axis=2, concat_axis=2, tiled=True)]
    scatter x4 -> x0, local copies, waits for them, and re-layouts: 25.1 us -> none  [the longest x2 12.9 us: pack_slots(): send_vals = jnp.zeros((values.shape[0], capacity, n_slab), jnp.float32).a...]
    all_to_all x2 -> x0, starting transfers between devices: 19.5 us -> none  [the longest x1 9.95 us: body(): lax.all_to_all(send_ids, 'slab', split_axis=2, concat_axis=2, tiled=True)]
    reshape x4 -> x0, local copies, waits for them, and re-layouts: 11.2 us -> none  [the longest x1 5.71 us: stiffness(): stacked = jnp.stack(corners, 0).reshape(24, -1)]
    ppermute x4 -> x0, starting transfers between devices: 9.3 us -> none  [the longest x2 5.11 us: extended(): before = lax.ppermute(last, axis, up)]
    dot_general x2 -> x0, matrix products: 7.56 us -> none  [the longest x1 6.87 us: stiffness(): jnp.dot(element_matrix, stacked, precision=lax.Precision.HIGHEST, preferr...]
  transfers between devices with their start and end apart: 6 -> 0, of which waited for: 3 -> 0; matrix products, arithmetic and copies ran while one was open for 4% -> 0% of each run, Pallas kernels for 0% -> 0%
where the time goes in v1:
time: 55.6 us; the launch traced here: 55.3 us
  Pallas kernels  48.5 us (87%)
  local copies, waits for them, and re-layouts  6.06 us (11%)
  between operations  0.67 us (1%)
    pallas_call x1, Pallas kernels, body(): pl.pallas_call(kernel, out_shape=(jax.ShapeDtypeStruct((24, ROWS, NY), F3...  48.5 us
    unnamed x18, local copies, waits for them, and re-layouts  6.06 us

profile of v1, /device:TPU:1, one launch (start us, length us, event | category | flops | bytes accessed | tf_op | source)
XLA Modules:
  0.0 55.3 jit_solution(3358728518867417542)
XLA Ops:
  0.6 0.0 copy-start.5
  0.6 0.0 copy-start.6
  0.7 0.0 copy-start.7
  0.7 0.7 %copy-done.5 = f32[3,1,256]{2,1,0:T(1,128)S(1)} copy-done((f32[3,1,256]{2,1,0:T(1,128)S(1)}, f32[3,1,256]{2,1,0:T(1,128)}, u32[]{:S(2)}) %copy-start.5) | copy-done | bytes 3096
  1.3 0.0 copy-done.6
  1.3 0.0 copy-done.7
  1.3 0.0 copy-start
  1.3 1.1 %copy-done = f32[384,384]{1,0:T(8,128)S(1)} copy-done((f32[384,384]{1,0:T(8,128)S(1)}, f32[384,384]{1,0:T(8,128)}, u32[]{:S(2)}) %copy-start) | copy-done | bytes 589848
  2.4 0.0 copy-start.1
  2.4 0.9 %copy-done.1 = f32[3,8,1,8,256]{4,3,2,1,0:T(8,128)S(1)} copy-done((f32[3,8,1,8,256]{4,3,2,1,0:T(8,128)S(1)}, f32[3,8,1,8,256]{4,3,2,1,0:T(8,128)}, u32[]{:S(2)}) %copy-start.1) | copy-done | bytes 196632
  3.3 0.0 copy-start.2
  3.3 0.7 %copy-done.2 = f32[3,1,8,256]{3,2,1,0:T(8,128)S(1)} copy-done((f32[3,1,8,256]{3,2,1,0:T(8,128)S(1)}, f32[3,1,8,256]{3,2,1,0:T(8,128)}, u32[]{:S(2)}) %copy-start.2) | copy-done | bytes 24600
  4.1 0.0 copy-start.3
  4.1 0.7 %copy-done.3 = f32[24,24]{1,0:T(8,128)S(1)} copy-done((f32[24,24]{1,0:T(8,128)S(1)}, f32[24,24]{1,0:T(8,128)}, u32[]{:S(2)}) %copy-start.3) | copy-done | bytes 2328
  4.8 0.0 copy-start.4
  4.8 0.7 %copy-done.4 = s32[1,8,256]{2,1,0:T(8,128)S(1)} copy-done((s32[1,8,256]{2,1,0:T(8,128)S(1)}, s32[1,8,256]{2,1,0:T(8,128)}, u32[]{:S(2)}) %copy-start.4) | copy-done | bytes 8216
  5.5 48.5 %shard_map.95 = (f32[24,8,256]{2,1,0:T(8,128)S(1)}, f32[2,256]{1,0:T(2,128)S(1)}) custom-call(f32[24,8,256]{2,1,0:T(8,128)S(1)} %bitcast.7, f32[3,8,256]{2,1,0:T(8,128)S(1)} %bitcast.8, s32[8,256]{1,0:T(8,128)S(1)} %bitcast.9, f32[16]{0:T(128)S(1)} %copy-done.7, f32[24,24]{1,0:T(8,128)S(1)} %copy-done.3, f32[384,384]{1,0:T(8,128)S(1)} %copy-done, ...), custom_call_target="tpu_custom_call" | custom-call | tf_op jit(solution)/shard_map/pallas_call | solution.py:415
  54.0 0.7 %copy.13 = f32[3,8,1,8,256]{4,3,2,1,0:T(8,128)} copy(f32[3,8,1,8,256]{4,3,2,1,0:T(8,128)S(1)} %bitcast.6) | data formatting | bytes 393216
  54.7 0.6 %copy.14 = f32[2,256]{1,0:T(2,128)} copy(f32[2,256]{1,0:T(2,128)S(1)} %get-tuple-element.11) | data formatting | bytes 4096
Async XLA Ops:
  0.6 0.7 %copy-start.5 = (f32[3,1,256]{2,1,0:T(1,128)S(1)}, f32[3,1,256]{2,1,0:T(1,128)}, u32[]{:S(2)}) copy-start(f32[3,1,256]{2,1,0:T(1,128)} %los_ref.1) | copy-start | bytes 9220
  0.6 0.7 %copy-start.6 = (s32[1,256]{1,0:T(1,128)S(1)}, s32[1,256]{1,0:T(1,128)}, u32[]{:S(2)}) copy-start(s32[1,256]{1,0:T(1,128)} %map_ref.1) | copy-start | bytes 3076
  0.7 0.7 %copy-start.7 = (f32[16]{0:T(128)S(1)}, f32[16]{0:T(128)}, u32[]{:S(2)}) copy-start(f32[16]{0:T(128)} %mod_ref.1) | copy-start | bytes 196
  1.3 1.1 %copy-start = (f32[384,384]{1,0:T(8,128)S(1)}, f32[384,384]{1,0:T(8,128)}, u32[]{:S(2)}) copy-start(f32[384,384]{1,0:T(8,128)} %c_ref.1) | copy-start | bytes 1769476
  2.4 0.9 %copy-start.1 = (f32[3,8,1,8,256]{4,3,2,1,0:T(8,128)S(1)}, f32[3,8,1,8,256]{4,3,2,1,0:T(8,128)}, u32[]{:S(2)}) copy-start(f32[3,8,1,8,256]{4,3,2,1,0:T(8,128)} %param.8) | copy-start | bytes 589828
  3.3 0.7 %copy-start.2 = (f32[3,1,8,256]{3,2,1,0:T(8,128)S(1)}, f32[3,1,8,256]{3,2,1,0:T(8,128)}, u32[]{:S(2)}) copy-start(f32[3,1,8,256]{3,2,1,0:T(8,128)} %param.9) | copy-start | bytes 73732
  4.1 0.7 %copy-start.3 = (f32[24,24]{1,0:T(8,128)S(1)}, f32[24,24]{1,0:T(8,128)}, u32[]{:S(2)}) copy-start(f32[24,24]{1,0:T(8,128)} %e_ref.1) | copy-start | bytes 6916
  4.8 0.7 %copy-start.4 = (s32[1,8,256]{2,1,0:T(8,128)S(1)}, s32[1,8,256]{2,1,0:T(8,128)}, u32[]{:S(2)}) copy-start(s32[1,8,256]{2,1,0:T(8,128)} %param.10) | copy-start | bytes 24580

commit v2 on v1

v2 whole, which is shorter than its diff:
```python
import jax
import jax.numpy as jnp
from jax import lax
from jax.experimental import pallas as pl
from jax.experimental.pallas import tpu as pltpu
from jax.sharding import PartitionSpec as P

F32, BF16 = jnp.float32, jnp.bfloat16
MESH = pl.DeviceIdType.MESH
HIGHEST = lax.Precision.HIGHEST
NX, NZ, NC, ND = 4, 16, 2, 4
SLABS, ROWS, NY = NX * NZ * NC, 8, 256
NODES = ROWS * ND * NY


def iota(shape, dim):
    return lax.broadcasted_iota(jnp.int32, shape, dim)


def dot(a, b):
    return jnp.dot(a, b, preferred_element_type=F32)


def dot_full(a, b):
    return jnp.dot(a, b, preferred_element_type=F32, precision=HIGHEST)


def dot_nt(a, b):
    return lax.dot_general(a, b, (((1,), (1,)), ((), ())), preferred_element_type=F32)


def split(v):
    high = v.astype(BF16)
    return high, (v - high.astype(F32)).astype(BF16)


def fsplit(v):
    high = v.astype(BF16).astype(F32)
    return high, v - high


def hot(mask):
    return jnp.where(mask, 1.0, 0.0).astype(F32)


def from_right(v):
    width = v.shape[1]
    return jnp.where(iota(v.shape, 1) == width - 1, 0.0, pltpu.roll(v, width - 1, axis=1))


def from_left(v):
    return jnp.where(iota(v.shape, 1) == 0, 0.0, pltpu.roll(v, 1, axis=1))


def to_row(columns):
    lane, sub = iota((8, 128), 1), iota((8, 128), 0)
    total = jnp.zeros((8, 128), F32)
    for q, column in enumerate(columns):
        total = jnp.where(lane == q * 8 + sub, column, total)
    return jnp.sum(total, axis=0, keepdims=True)


def pick_row(v, index):
    return jnp.sum(jnp.where(iota(v.shape, 0) == index, v, 0.0), axis=0, keepdims=True)


def kernel(
    r_hbm, s_hbm, mat_hbm, mod_ref, e_hbm, c_hbm, map_hbm, los_hbm,
    res_ref, pix_ref,
    r_ref, s_ref, mat_ref, e_ref, c_ref, map_ref, los_ref,
    rt, st, hp, hz, own_mod, mod_in, mods, w, f_own, lhs_own, lhs_nb, app, g_z,
    c_perm, pj_out, pj_in, px_out, px_mid, px_in, gps,
    y_out, y_in, z_out, z_in, all_in,
    load, send, recv,
):
    s, d = lax.axis_index("slab"), lax.axis_index("depth")
    x, z, c = s // 32, (s // 2) % 16, s % 2
    g = x * 2 + c
    half = g // 4
    up, down = lax.rem(s + 1, SLABS), lax.rem(s + SLABS - 1, SLABS)
    deeper, higher = lax.rem(d + 1, ND), lax.rem(d + ND - 1, ND)

    y_peers = [(s, lax.rem(d + i, ND)) for i in range(1, ND)]
    z_ids = [lax.rem(z + i, NZ) for i in range(1, NZ)]
    z_peers = [(x * 32 + i * 2 + c, d) for i in z_ids]
    g_ids = [lax.rem(g + i, 8) for i in range(1, 8)]
    g_peers = [((i // 2) * 32 + z * 2 + i % 2, d) for i in g_ids]
    near = [(up, d), (down, d)] + [(a, b) for a in (up, down) for b in (deeper, higher)]

    barrier = pltpu.get_barrier_semaphore()
    peers = z_peers + near + y_peers + g_peers
    for peer in peers:
        pl.semaphore_signal(barrier, inc=1, device_id=peer, device_id_type=MESH)

    pairs = [
        (r_hbm, r_ref), (s_hbm, s_ref), (mat_hbm, mat_ref), (los_hbm, los_ref),
        (map_hbm, map_ref), (e_hbm, e_ref), (c_hbm, c_ref),
    ]
    loads = [pltpu.make_async_copy(a, b, load.at[i]) for i, (a, b) in enumerate(pairs)]
    for each in loads:
        each.start()

    def copy(src, dst, index, peer):
        return pltpu.make_async_remote_copy(
            src_ref=src, dst_ref=dst, send_sem=send.at[index], recv_sem=recv.at[index],
            device_id=peer, device_id_type=MESH,
        )

    loads[0].wait()
    loads[1].wait()
    field = jnp.transpose(r_ref[...], (1, 0, 2))
    rt[...] = field
    for k in range(ROWS):
        weight = jnp.concatenate(
            [jnp.broadcast_to(s_ref[m, k : k + 1, :], (8, NY)) for m in range(3)], axis=0
        )
        st[k] = field[k] * weight
    loads[2].wait()
    material = mat_ref[...]
    modulus = jnp.zeros((ROWS, NY), F32)
    for i in range(16):
        modulus = jnp.where(material == i, mod_ref[i], modulus)
    own_mod[...] = modulus
    loads[3].wait()
    shown = jnp.zeros((8, NY), F32)
    for m in range(3):
        shown = shown + los_ref[m] * st[ROWS - 1, m * 8 : m * 8 + 8, :]
    pj_out[...] = shown

    pl.semaphore_wait(barrier, len(peers))

    started = []
    for i, peer in enumerate([(down, d), (s, higher), (down, higher)]):
        started.append(copy(own_mod, mod_in.at[i], 3 + i, peer))
        started[-1].start()
    sides = []
    for plane, a in ((1, s), (2, down), (0, up)):
        sides.append((st.at[0], hz.at[plane, 1], (a, higher)))
        sides.append((st.at[ROWS - 1], hz.at[plane, 0], (a, deeper)))
    for i, (src, dst, peer) in enumerate(sides):
        started.append(copy(src, dst, 9 + i, peer))
        started[-1].start()
    for i, (plane, peer) in enumerate(((1, (down, d)), (0, (up, d)))):
        started.append(copy(st, hp.at[plane], 15 + i, peer))
        started[-1].start()

    def shows():
        return [copy(pj_out, pj_in, 6 + i, (s, i)) for i in range(ND - 1)]

    @pl.when(d == ND - 1)
    def _():
        for each in shows():
            each.start()
        pj_in[...] = shown

    block_sum = jnp.zeros((24, NY), F32)
    force_sum = jnp.zeros((24, NY), F32)
    for k in range(ROWS):
        block_sum = block_sum + rt[k]
        force_sum = force_sum + rt[k] * st[k]
    block_sum = jnp.sum(block_sum, axis=1, keepdims=True)
    force_sum = jnp.sum(force_sum, axis=1, keepdims=True)

    loads[5].wait()
    e = e_ref[...]
    rho, eps = iota((192, 24), 0), iota((192, 24), 1)
    picked = dot_full(hot(eps == (rho % 96) // 8 + 12 * (1 - rho // 96)), e)
    eps, kap = iota((24, 192), 0), iota((24, 192), 1)
    column = 6 * (kap // 96) + (kap % 48) // 8
    wide = [dot_full(picked, hot(eps == column + 12 * a)) for a in range(2)]
    rho, kap = iota((96, 192), 0), iota((96, 192), 1)
    same_source = rho % 8 == kap % 8
    first = same_source & (kap % 96 < 48)
    parts = [wide[1][:96], wide[0][96:], wide[0][:96], wide[1][96:]]
    for i, part in enumerate(parts):
        high, low = fsplit(part)
        high = jnp.where(same_source, high, 0.0).astype(BF16)
        low = jnp.where(first, low, 0.0).astype(BF16)
        if i < 2:
            lhs_own[0, i * 96 : i * 96 + 96] = high
            lhs_own[1, i * 96 : i * 96 + 96] = low
        else:
            lhs_nb[i - 2, 0] = high
            lhs_nb[i - 2, 1] = low

    loads[4].wait()
    target = map_ref[...]
    tile, in_tile = target >> 8, target & 255
    tile_col = jnp.transpose(jnp.broadcast_to(tile.astype(F32), (8, NY)))[:, 0:1]
    same = (tile_col == tile.astype(F32)) & (iota((NY, NY), 0) < iota((NY, NY), 1))
    rank = jnp.sum(hot(same), axis=0, keepdims=True).astype(jnp.int32)
    tile_g = (tile >> 5) * 2 + (tile & 1)
    place_row = (tile_g >> 2) * 16 + ((tile >> 1) & 15)
    place_lane = (tile_g & 3) * 32 + rank
    row_hot = hot(iota((32, NY), 0) == place_row)

    @pl.when(d != ND - 1)
    def _():
        copy(pj_out, pj_in, 6 + d, (s, d)).wait_recv()

    shown = pj_in[...]
    values = [pick_row(shown, 2 * d), pick_row(shown, 2 * d + 1)]
    values += [los_ref[m] for m in range(3)] + [in_tile.astype(F32)]
    packed = jnp.zeros((64, 128), F32)
    for v, value in enumerate(values):
        high, low = fsplit(value)
        left = jnp.concatenate([row_hot * high, row_hot * low], axis=0).astype(BF16)
        right = hot(iota((128, NY), 0) == place_lane + 4 * v).astype(BF16)
        packed = packed + dot_nt(left, right)
    packed = packed[:32] + packed[32:]
    px_out[:, 0] = packed[:16].reshape(16, 1, 128)
    px_out[:, 1] = packed[16:].reshape(16, 1, 128)
    px_mid[z] = px_out[z]
    for i, peer in enumerate(z_peers):
        started.append(copy(px_out.at[z_ids[i]], px_mid.at[z], 17 + i, peer))
        started[-1].start()

    def weave(plane, index, value, alive):
        if alive is not None:
            value = jnp.where(alive, value, 0.0)
        high, low = split(jnp.concatenate([from_left(value), value], axis=0))
        w[plane, index * 96 : index * 96 + 48] = high
        w[plane, index * 96 + 48 : index * 96 + 96] = low

    for k in range(ROWS):
        weave(1, k + 1, st[k], None)

    for i in range(3):
        copy(own_mod, mod_in.at[i], 3 + i, (down, d)).wait_recv()
    inner = d < ND - 1
    last = s == SLABS - 1
    for k in range(ROWS):
        mods[0, k] = own_mod[k : k + 1, :]
        mods[1, k] = jnp.where(last, 0.0, mod_in[0, k : k + 1, :])
    mods[0, ROWS] = jnp.where(inner, mod_in[1, 0:1, :], 0.0)
    mods[1, ROWS] = jnp.where(inner & jnp.logical_not(last), mod_in[2, 0:1, :], 0.0)

    rho, eps = iota((128, 24), 0), iota((128, 24), 1)
    corner, rest = rho // 32, rho % 32
    comp, plane, comp2 = rest // 9, (rest % 9) // 3, rest % 3
    left = jnp.zeros((128, 8), F32)
    for layer in range(2):
        rows = dot_full(hot((eps == 12 * (1 - layer) + 3 * corner + comp) & (rest < 27)), e)
        keep = (eps % 3 == comp2) & (eps // 12 == plane - layer)
        of, to = iota((24, 8), 0), iota((24, 8), 1)
        gather = hot((to // 4 == layer) & ((of % 12) // 3 == to % 4))
        left = left + dot_full(jnp.where(keep, rows, 0.0), gather)
    high, low = fsplit(left)
    left_high = jnp.concatenate([high, high], axis=1).astype(BF16)
    left_low = jnp.concatenate([low, jnp.zeros_like(low)], axis=1).astype(BF16)
    before = None
    unit_sum = jnp.zeros((32, NY), F32)
    for k in range(ROWS + 1):
        sub, lane = iota((8, NY), 0), iota((8, NY), 1)
        block = jnp.where(sub < 4, mods[0, k], mods[1, k])
        there = (sub % 2 == 1) | (lane > 0)
        if k == 0:
            there = there & ((sub % 4 >= 2) | (d > 0))
        block = jnp.where(there, block, 0.0)
        high, low = fsplit(block)
        block = jnp.concatenate([high, low], axis=0).astype(BF16)
        now = dot(left_high, block) + dot(left_low, block)
        if before is not None:
            both = before[64:] + now[:64]
            both = both[32:] + from_right(both[:32])
            g_z[k - 1] = both
            unit_sum = unit_sum + both
        before = now
    unit_sum = jnp.sum(unit_sum, axis=1, keepdims=True)

    for i in range(6):
        copy(st.at[0], hz.at[0, 0], 9 + i, (s, higher)).wait_recv()
    not_first, not_last = s > 0, s < SLABS - 1
    weave(1, 0, hz[1, 0], d > 0)
    weave(1, 9, hz[1, 1], inner)
    for k in range(ROWS + 1):
        block = w[1, 96 * k : 96 * k + 192]
        f = dot(lhs_own[0], block) + dot(lhs_own[1], block)
        f_own[k] = mods[0, k] * f[:96] + mods[1, k] * f[96:]

    for i in range(2):
        copy(st, hp.at[i], 15 + i, (down, d)).wait_recv()
    for plane, index, alive in ((0, 0, not_first), (2, 1, not_last)):
        weave(plane, 0, hz[plane, 0], alive & (d > 0))
        weave(plane, 9, hz[plane, 1], alive & inner)
        for k in range(ROWS):
            weave(plane, k + 1, hp[index, k], alive)
    before = None
    near_sum = jnp.zeros((24, NY), F32)
    cross_sum = jnp.zeros((24, NY), F32)
    for k in range(ROWS + 1):
        now = f_own[k]
        for i in range(2):
            block = w[2 * i, 96 * k : 96 * k + 192]
            now = now + mods[i, k] * (dot(lhs_nb[i, 0], block) + dot(lhs_nb[i, 1], block))
        if before is not None:
            both = before[48:] + now[:48]
            both = both[24:] + from_right(both[:24])
            app[k - 1] = both
            near_sum = near_sum + both * st[k - 1]
            cross_sum = cross_sum + both
        before = now
    near_sum = jnp.sum(near_sum, axis=1, keepdims=True)
    cross_sum = jnp.sum(cross_sum, axis=1, keepdims=True)

    def thirds(v):
        return [v[m * 8 : m * 8 + 8] for m in range(3)]

    row = to_row(
        thirds(block_sum)
        + [sum(thirds(force_sum)), sum(thirds(near_sum))]
        + thirds(cross_sum)
        + [unit_sum[i * 8 : i * 8 + 8] for i in range(4)]
    )
    y_out[...] = row
    y_in[d] = row
    for i, peer in enumerate(y_peers):
        started.append(copy(y_out, y_in.at[d], i, peer))
        started[-1].start()

    for i in range(15):
        copy(px_out.at[0], px_mid.at[0], 17 + i, (down, d)).wait_recv()
    for i, peer in enumerate(g_peers):
        started.append(copy(px_mid.at[:, g_ids[i] // 4], px_in.at[x, :, c], 32 + i, peer))
        started[-1].start()
    for k in range(NZ):
        px_in[x, k, c] = px_mid[k, half]

    for i in range(3):
        copy(y_out, y_in.at[0], i, y_peers[i]).wait_recv()
    row = y_in[0] + y_in[1] + y_in[2] + y_in[3]
    z_out[...] = row
    z_in[z] = row
    for i, peer in enumerate(z_peers):
        started.append(copy(z_out, z_in.at[z], 39 + i, peer))
        started[-1].start()

    loads[6].wait()
    order = hot(iota((384, 384), 0) == 3 * (iota((384, 384), 1) % 128) + iota((384, 384), 1) // 128)
    order_t = hot(iota((384, 384), 1) == 3 * (iota((384, 384), 0) % 128) + iota((384, 384), 0) // 128)
    order, order_t = order.astype(BF16), order_t.astype(BF16)
    for i, part in enumerate(split(c_ref[...])):
        c_perm[i] = dot(order_t, dot(part, order).astype(BF16)).astype(BF16)

    for i in range(7):
        copy(px_mid.at[:, 0], px_in.at[0, :, 0], 32 + i, (down, d)).wait_recv()
    gps[...] = jnp.transpose(px_in.reshape(SLABS, 128)[...])
    group = gps[pl.ds(pl.multiple_of((g % 4) * 32, 32), 32), :]
    ids = group[20:24].astype(jnp.int32)
    bins_right = jnp.concatenate(
        [hot(iota((256, 128), 0) == ids[j : j + 1]) for j in range(4)], axis=1
    ).astype(BF16)

    for i in range(15):
        copy(z_out, z_in.at[0], 39 + i, (down, d)).wait_recv()
    for i, peer in enumerate(g_peers):
        started.append(copy(z_in, all_in.at[x, :, c], 54 + i, peer))
        started[-1].start()
    for k in range(NZ):
        all_in[x, k, c] = z_in[k]
    for i in range(7):
        copy(z_in, all_in.at[0, :, 0], 54 + i, (down, d)).wait_recv()

    slabs = jnp.transpose(all_in.reshape(SLABS, 128)[...])
    sums = [slabs[q * 8 : q * 8 + 8] for q in range(8)]
    means = jnp.concatenate(sums[:3], axis=1) * (1.0 / NODES)
    high, low = fsplit(means)
    both = jnp.concatenate([high, low], axis=0).astype(BF16)
    solved = dot(both, c_perm[0])
    corr = solved[:8] + solved[8:] + dot(both, c_perm[1])[:8]
    corr = [corr[:, m * 128 : m * 128 + 128] for m in range(3)]

    shifted = [[from_left(v) for v in corr], corr, [from_right(v) for v in corr]]
    numerator, denominator = sums[3], sums[4]
    for m in range(3):
        numerator = numerator + corr[m] * sums[m]
        part = 2.0 * sums[5 + m]
        for p in range(3):
            for m2 in range(3):
                i = 64 + m * 9 + p * 3 + m2
                part = part + slabs[i : i + 1] * shifted[p][m2]
        denominator = denominator + corr[m] * part
    step = jnp.sum(numerator, axis=1, keepdims=True) / jnp.sum(denominator, axis=1, keepdims=True)
    lane = iota((8, 128), 1)
    mine = [
        [jnp.sum(jnp.where(lane == s, v, 0.0), axis=1, keepdims=True) for v in shifted[p]]
        for p in range(3)
    ]
    steps = jnp.concatenate([step] * 3, axis=0)
    for k in range(ROWS):
        grown = []
        for m in range(3):
            total = app[k, m * 8 : m * 8 + 8]
            for p in range(3):
                for m2 in range(3):
                    i = m * 9 + p * 3 + m2
                    total = total + mine[p][m2] * g_z[k, i : i + 1]
            grown.append(total)
        app[k] = rt[k] - steps * jnp.concatenate(grown, axis=0)
    res_ref[...] = jnp.transpose(app[...], (1, 0, 2))

    found = []
    for v in range(2):
        value = group[4 * v : 4 * v + 4]
        for m in range(3):
            value = value + group[8 + 4 * m : 12 + 4 * m] * pick_row(corr[m], 2 * d + v)
        found.append(jnp.concatenate([value[j : j + 1] for j in range(4)], axis=1))
    sub = iota((8, 512), 0)
    parts = [fsplit(v) for v in found]
    left = jnp.where(sub == 0, parts[0][0], jnp.where(sub == 1, parts[1][0], 0.0))
    left = jnp.where(sub == 2, parts[0][1], jnp.where(sub == 3, parts[1][1], left))
    bins = dot_nt(left.astype(BF16), bins_right)
    wide_step = jnp.broadcast_to(step, (8, NY))
    for v in range(2):
        pix_ref[v : v + 1, :] = pick_row(wide_step, 2 * d + v) * (
            bins[v : v + 1] + bins[v + 2 : v + 3]
        )

    for each in started:
        each.wait_send()

    @pl.when(d == ND - 1)
    def _():
        for each in shows():
            each.wait_send()


def body(right_side, smoother, material, moduli, element_matrix, coarse_inverse, surface_map, line_of_sight):
    vmem = pl.BlockSpec(memory_space=pltpu.VMEM)
    smem = pl.BlockSpec(memory_space=pltpu.SMEM)
    hbm = pl.BlockSpec(memory_space=pltpu.HBM)
    residual, pixels = pl.pallas_call(
        kernel,
        out_shape=(
            jax.ShapeDtypeStruct((24, ROWS, NY), F32),
            jax.ShapeDtypeStruct((2, NY), F32),
        ),
        in_specs=[hbm, hbm, hbm, smem, hbm, hbm, hbm, hbm],
        out_specs=(vmem, vmem),
        scratch_shapes=[
            pltpu.VMEM((24, ROWS, NY), F32),
            pltpu.VMEM((3, ROWS, NY), F32),
            pltpu.VMEM((ROWS, NY), jnp.int32),
            pltpu.VMEM((24, 24), F32),
            pltpu.VMEM((384, 384), F32),
            pltpu.VMEM((1, NY), jnp.int32),
            pltpu.VMEM((3, 1, NY), F32),
            pltpu.VMEM((ROWS, 24, NY), F32),
            pltpu.VMEM((ROWS, 24, NY), F32),
            pltpu.VMEM((2, ROWS, 24, NY), F32),
            pltpu.VMEM((3, 2, 24, NY), F32),
            pltpu.VMEM((ROWS, NY), F32),
            pltpu.VMEM((3, ROWS, NY), F32),
            pltpu.VMEM((2, ROWS + 1, 1, NY), F32),
            pltpu.VMEM((3, 960, NY), BF16),
            pltpu.VMEM((ROWS + 1, 96, NY), F32),
            pltpu.VMEM((2, 192, 192), BF16),
            pltpu.VMEM((2, 2, 96, 192), BF16),
            pltpu.VMEM((ROWS, 24, NY), F32),
            pltpu.VMEM((ROWS, 32, NY), F32),
            pltpu.VMEM((2, 384, 384), BF16),
            pltpu.VMEM((8, NY), F32),
            pltpu.VMEM((8, NY), F32),
            pltpu.VMEM((NZ, 2, 1, 128), F32),
            pltpu.VMEM((NZ, 2, 1, 128), F32),
            pltpu.VMEM((NX, NZ, NC, 1, 128), F32),
            pltpu.VMEM((128, 128), F32),
            pltpu.VMEM((1, 128), F32),
            pltpu.VMEM((ND, 1, 128), F32),
            pltpu.VMEM((1, 128), F32),
            pltpu.VMEM((NZ, 1, 128), F32),
            pltpu.VMEM((NX, NZ, NC, 1, 128), F32),
            pltpu.SemaphoreType.DMA((7,)),
            pltpu.SemaphoreType.DMA((61,)),
            pltpu.SemaphoreType.DMA((61,)),
        ],
        compiler_params=pltpu.CompilerParams(
            collective_id=0, has_side_effects=True, vmem_limit_bytes=60 * 1024 * 1024
        ),
    )(
        right_side.reshape(24, ROWS, NY),
        smoother.reshape(3, ROWS, NY),
        material.reshape(ROWS, NY),
        moduli,
        element_matrix,
        coarse_inverse,
        surface_map,
        line_of_sight,
    )
    return residual.reshape(right_side.shape), pixels


def solution(mesh):
    return jax.shard_map(
        body,
        mesh=mesh,
        in_specs=(
            P(None, None, "slab", "depth", None),
            P(None, "slab", "depth", None),
            P("slab", "depth", None),
            P(),
            P(),
            P(),
            P("slab", None),
            P(None, "slab", None),
        ),
        out_specs=(P(None, None, "slab", "depth", None), P("depth", "slab")),
        check_vma=False,
    )
```

time: 55.6 us -> 46.4 us (0.83)
  Pallas kernels: 48.5 us -> 43.4 us
  local copies, waits for them, and re-layouts: 6.06 us -> 2.2 us
    pallas_call x1, Pallas kernels: 48.5 us -> 43.4 us  [body(): pl.pallas_call(kernel, out_shape=(jax.ShapeDtypeStruct((24, ROWS, NY), F3...]
    unnamed x18 -> x4, local copies, waits for them, and re-layouts: 6.06 us -> 2.2 us
where the time goes in v2:
time: 46.4 us; the launch traced here: 46.2 us
  Pallas kernels  43.4 us (94%)
  local copies, waits for them, and re-layouts  2.2 us (5%)
  between operations  0.65 us (1%)
    pallas_call x1, Pallas kernels, body(): pl.pallas_call(kernel, out_shape=(jax.ShapeDtypeStruct((24, ROWS, NY), F3...  43.4 us
    unnamed x4, local copies, waits for them, and re-layouts  2.2 us

profile of v2, /device:TPU:1, one launch (start us, length us, event | category | flops | bytes accessed | tf_op | source)
XLA Modules:
  0.0 46.2 jit_solution(14654151123460495301)
XLA Ops:
  0.6 43.4 %shard_map.95 = (f32[24,8,256]{2,1,0:T(8,128)}, f32[2,256]{1,0:T(2,128)}) custom-call(f32[24,8,256]{2,1,0:T(8,128)} %bitcast.7, f32[3,8,256]{2,1,0:T(8,128)} %bitcast.8, s32[8,256]{1,0:T(8,128)} %bitcast.9, f32[16]{0:T(128)} %mod_ref.1, f32[24,24]{1,0:T(8,128)} %e_hbm.1, f32[384,384]{1,0:T(8,128)} %c_hbm.1, s32[1,256]{1,0:T(1,128)} %map_hbm.1, ...), custom_call_target="tpu_custom_call" | custom-call | tf_op jit(solution)/shard_map/pallas_call | solution.py:432
  44.0 0.0 copy-start
  44.0 1.6 %copy.13 = f32[3,8,1,8,256]{4,3,2,1,0:T(8,128)} copy(f32[3,8,1,8,256]{4,3,2,1,0:T(8,128)} %bitcast.6) | data formatting | bytes 393216
  45.6 0.0 copy-done
  45.6 0.6 %copy.14 = f32[2,256]{1,0:T(2,128)} copy(f32[2,256]{1,0:T(2,128)S(1)} %copy-done) | data formatting | bytes 4096
Async XLA Ops:
  44.0 1.6 %copy-start = (f32[2,256]{1,0:T(2,128)S(1)}, f32[2,256]{1,0:T(2,128)}, u32[]{:S(2)}) copy-start(f32[2,256]{1,0:T(2,128)} %get-tuple-element.11) | copy-start | bytes 6148

commit v3 on v2

--- a/solution.py
+++ b/solution.py
@@ -69,8 +69,8 @@
     res_ref, pix_ref,
     r_ref, s_ref, mat_ref, e_ref, c_ref, map_ref, los_ref,
     rt, st, hp, hz, own_mod, mod_in, mods, w, f_own, lhs_own, lhs_nb, app, g_z,
-    c_perm, pj_out, pj_in, px_out, px_mid, px_in, gps,
-    y_out, y_in, z_out, z_in, all_in,
+    c_perm, pj_out, pj_in, px_out, px_raw, px_relay, px_mid, px_in, ordered, gps,
+    y_out, y_in, z_out, all_in,
     load, send, recv,
 ):
     s, d = lax.axis_index("slab"), lax.axis_index("depth")
@@ -80,15 +80,19 @@
     up, down = lax.rem(s + 1, SLABS), lax.rem(s + SLABS - 1, SLABS)
     deeper, higher = lax.rem(d + 1, ND), lax.rem(d + ND - 1, ND)
 
-    y_peers = [(s, lax.rem(d + i, ND)) for i in range(1, ND)]
-    z_ids = [lax.rem(z + i, NZ) for i in range(1, NZ)]
-    z_peers = [(x * 32 + i * 2 + c, d) for i in z_ids]
+    z_id = {j: lax.rem(z + j + NZ, NZ) for j in range(-8, 9)}
+    z_steps = [1, 2, 3, 4, -1, -2, -3, -4]
+    z_peer = {j: (x * 32 + z_id[j] * 2 + c, d) for j in z_steps}
     g_ids = [lax.rem(g + i, 8) for i in range(1, 8)]
     g_peers = [((i // 2) * 32 + z * 2 + i % 2, d) for i in g_ids]
+    layer_peers = []
+    for i in range(1, 32):
+        h = lax.rem(g + i // ND, 8)
+        layer_peers.append(((h // 2) * 32 + z * 2 + h % 2, lax.rem(d + i % ND, ND)))
     near = [(up, d), (down, d)] + [(a, b) for a in (up, down) for b in (deeper, higher)]
 
     barrier = pltpu.get_barrier_semaphore()
-    peers = z_peers + near + y_peers + g_peers
+    peers = list(z_peer.values()) + near + layer_peers
     for peer in peers:
         pl.semaphore_signal(barrier, inc=1, device_id=peer, device_id_type=MESH)
 
@@ -194,6 +198,8 @@
     place_lane = (tile_g & 3) * 32 + rank
     row_hot = hot(iota((32, NY), 0) == place_row)
 
+    far = [5, 6, 7, 8, -5, -6, -7]
+
     @pl.when(d != ND - 1)
     def _():
         copy(pj_out, pj_in, 6 + d, (s, d)).wait_recv()
@@ -210,9 +216,13 @@
     packed = packed[:32] + packed[32:]
     px_out[:, 0] = packed[:16].reshape(16, 1, 128)
     px_out[:, 1] = packed[16:].reshape(16, 1, 128)
-    px_mid[z] = px_out[z]
-    for i, peer in enumerate(z_peers):
-        started.append(copy(px_out.at[z_ids[i]], px_mid.at[z], 17 + i, peer))
+    px_raw[z] = px_out[z]
+    for i, j in enumerate(z_steps):
+        started.append(copy(px_out.at[z_id[j]], px_raw.at[z], 17 + i, z_peer[j]))
+        started[-1].start()
+    for i, j in enumerate(far):
+        peer = z_peer[4 if j > 0 else -4]
+        started.append(copy(px_out.at[z_id[j]], px_relay.at[i], 25 + i, peer))
         started[-1].start()
 
     def weave(plane, index, value, alive):
@@ -278,6 +288,13 @@
         f = dot(lhs_own[0], block) + dot(lhs_own[1], block)
         f_own[k] = mods[0, k] * f[:96] + mods[1, k] * f[96:]
 
+    for i in range(7):
+        copy(px_out.at[0], px_relay.at[0], 25 + i, (down, d)).wait_recv()
+    for i, j in enumerate(far):
+        origin, peer = (z_id[-4], z_peer[j - 4]) if j > 0 else (z_id[4], z_peer[j + 4])
+        started.append(copy(px_relay.at[i], px_raw.at[origin], 39 + i, peer))
+        started[-1].start()
+
     for i in range(2):
         copy(st, hp.at[i], 15 + i, (down, d)).wait_recv()
     for plane, index, alive in ((0, 0, not_first), (2, 1, not_last)):
@@ -313,26 +330,30 @@
         + [unit_sum[i * 8 : i * 8 + 8] for i in range(4)]
     )
     y_out[...] = row
-    y_in[d] = row
-    for i, peer in enumerate(y_peers):
-        started.append(copy(y_out, y_in.at[d], i, peer))
-        started[-1].start()
-
-    for i in range(15):
-        copy(px_out.at[0], px_mid.at[0], 17 + i, (down, d)).wait_recv()
+    y_in[g, d] = row
+    for i, peer in enumerate(layer_peers):
+        started.append(copy(y_out, y_in.at[g, d], 61 + i, peer))
+        started[-1].start()
+
+    for i in range(8):
+        copy(px_out.at[0], px_raw.at[0], 17 + i, (down, d)).wait_recv()
+    for i in range(7):
+        copy(px_relay.at[0], px_raw.at[0], 39 + i, (down, d)).wait_recv()
+    pairs = px_raw.reshape(2 * NZ, 128)
+    for i in range(2):
+        px_mid[i] = pairs[pl.ds(i, NZ, stride=2), :]
     for i, peer in enumerate(g_peers):
-        started.append(copy(px_mid.at[:, g_ids[i] // 4], px_in.at[x, :, c], 32 + i, peer))
-        started[-1].start()
-    for k in range(NZ):
-        px_in[x, k, c] = px_mid[k, half]
-
-    for i in range(3):
-        copy(y_out, y_in.at[0], i, y_peers[i]).wait_recv()
-    row = y_in[0] + y_in[1] + y_in[2] + y_in[3]
-    z_out[...] = row
-    z_in[z] = row
-    for i, peer in enumerate(z_peers):
-        started.append(copy(z_out, z_in.at[z], 39 + i, peer))
+        started.append(copy(px_mid.at[g_ids[i] // 4], px_in.at[g], 32 + i, peer))
+        started[-1].start()
+    px_in[g] = px_mid[half]
+
+    for i in range(31):
+        copy(y_out, y_in.at[0, 0], 61 + i, (down, d)).wait_recv()
+    rows = y_in[:, 0] + y_in[:, 1] + y_in[:, 2] + y_in[:, 3]
+    z_out[...] = rows
+    all_in[z] = rows
+    for i, j in enumerate(z_steps):
+        started.append(copy(z_out, all_in.at[z], 46 + i, z_peer[j]))
         started[-1].start()
 
     loads[6].wait()
@@ -343,25 +364,29 @@
         c_perm[i] = dot(order_t, dot(part, order).astype(BF16)).astype(BF16)
 
     for i in range(7):
-        copy(px_mid.at[:, 0], px_in.at[0, :, 0], 32 + i, (down, d)).wait_recv()
-    gps[...] = jnp.transpose(px_in.reshape(SLABS, 128)[...])
+        copy(px_mid.at[0], px_in.at[0], 32 + i, (down, d)).wait_recv()
+    for i in range(8):
+        ordered[0, pl.ds((i // 2) * 32 + i % 2, NZ, stride=2), :] = px_in[i]
+    gps[...] = jnp.transpose(ordered[0])
     group = gps[pl.ds(pl.multiple_of((g % 4) * 32, 32), 32), :]
     ids = group[20:24].astype(jnp.int32)
     bins_right = jnp.concatenate(
         [hot(iota((256, 128), 0) == ids[j : j + 1]) for j in range(4)], axis=1
     ).astype(BF16)
 
-    for i in range(15):
-        copy(z_out, z_in.at[0], 39 + i, (down, d)).wait_recv()
-    for i, peer in enumerate(g_peers):
-        started.append(copy(z_in, all_in.at[x, :, c], 54 + i, peer))
-        started[-1].start()
-    for k in range(NZ):
-        all_in[x, k, c] = z_in[k]
+    for i in range(8):
+        copy(z_out, all_in.at[0], 46 + i, (down, d)).wait_recv()
+    for i, j in enumerate([1, 2, 3, 4, -1, -2, -3]):
+        block = all_in.at[z_id[j]]
+        started.append(copy(block, block, 54 + i, z_peer[-4 if j > 0 else 4]))
+        started[-1].start()
     for i in range(7):
-        copy(z_in, all_in.at[0, :, 0], 54 + i, (down, d)).wait_recv()
-
-    slabs = jnp.transpose(all_in.reshape(SLABS, 128)[...])
+        copy(z_out, all_in.at[0], 54 + i, (down, d)).wait_recv()
+
+    gathered = all_in.reshape(SLABS, 128)
+    for i in range(8):
+        ordered[1, pl.ds((i // 2) * 32 + i % 2, NZ, stride=2), :] = gathered[pl.ds(i, NZ, stride=8), :]
+    slabs = jnp.transpose(ordered[1])
     sums = [slabs[q * 8 : q * 8 + 8] for q in range(8)]
     means = jnp.concatenate(sums[:3], axis=1) * (1.0 / NODES)
     high, low = fsplit(means)
@@ -463,16 +488,18 @@
             pltpu.VMEM((8, NY), F32),
             pltpu.VMEM((NZ, 2, 1, 128), F32),
             pltpu.VMEM((NZ, 2, 1, 128), F32),
-            pltpu.VMEM((NX, NZ, NC, 1, 128), F32),
+            pltpu.VMEM((7, 2, 1, 128), F32),
+            pltpu.VMEM((2, NZ, 128), F32),
+            pltpu.VMEM((8, NZ, 128), F32),
+            pltpu.VMEM((2, SLABS, 128), F32),
             pltpu.VMEM((128, 128), F32),
             pltpu.VMEM((1, 128), F32),
-            pltpu.VMEM((ND, 1, 128), F32),
-            pltpu.VMEM((1, 128), F32),
-            pltpu.VMEM((NZ, 1, 128), F32),
-            pltpu.VMEM((NX, NZ, NC, 1, 128), F32),
+            pltpu.VMEM((8, ND, 1, 128), F32),
+            pltpu.VMEM((8, 1, 128), F32),
+            pltpu.VMEM((NZ, 8, 1, 128), F32),
             pltpu.SemaphoreType.DMA((7,)),
-            pltpu.SemaphoreType.DMA((61,)),
-            pltpu.SemaphoreType.DMA((61,)),
+            pltpu.SemaphoreType.DMA((92,)),
+            pltpu.SemaphoreType.DMA((92,)),
         ],
         compiler_params=pltpu.CompilerParams(
             collective_id=0, has_side_effects=True, vmem_limit_bytes=60 * 1024 * 1024

time: 46.4 us -> 45.1 us (0.972)
  Pallas kernels: 43.4 us -> 41.9 us
    pallas_call x1, Pallas kernels: 43.4 us -> 41.9 us  [body(): pl.pallas_call(kernel, out_shape=(jax.ShapeDtypeStruct((24, ROWS, NY), F3...]
where the time goes in v3:
time: 45.1 us; the launch traced here: 44.8 us
  Pallas kernels  41.9 us (93%)
  local copies, waits for them, and re-layouts  2.2 us (5%)
  between operations  0.65 us (1%)
    pallas_call x1, Pallas kernels, body(): pl.pallas_call(kernel, out_shape=(jax.ShapeDtypeStruct((24, ROWS, NY), F3...  41.9 us
    unnamed x4, local copies, waits for them, and re-layouts  2.2 us

profile of v3, /device:TPU:1, one launch (start us, length us, event | category | flops | bytes accessed | tf_op | source)
XLA Modules:
  0.0 44.8 jit_solution(12895211250337976800)
XLA Ops:
  0.6 41.9 %shard_map.95 = (f32[24,8,256]{2,1,0:T(8,128)}, f32[2,256]{1,0:T(2,128)}) custom-call(f32[24,8,256]{2,1,0:T(8,128)} %bitcast.7, f32[3,8,256]{2,1,0:T(8,128)} %bitcast.8, s32[8,256]{1,0:T(8,128)} %bitcast.9, f32[16]{0:T(128)} %mod_ref.1, f32[24,24]{1,0:T(8,128)} %e_hbm.1, f32[384,384]{1,0:T(8,128)} %c_hbm.1, s32[1,256]{1,0:T(1,128)} %map_hbm.1, ...), custom_call_target="tpu_custom_call" | custom-call | tf_op jit(solution)/shard_map/pallas_call | solution.py:457
  42.6 0.0 copy-start
  42.6 1.6 %copy.13 = f32[3,8,1,8,256]{4,3,2,1,0:T(8,128)} copy(f32[3,8,1,8,256]{4,3,2,1,0:T(8,128)} %bitcast.6) | data formatting | bytes 393216
  44.2 0.0 copy-done
  44.2 0.6 %copy.14 = f32[2,256]{1,0:T(2,128)} copy(f32[2,256]{1,0:T(2,128)S(1)} %copy-done) | data formatting | bytes 4096
Async XLA Ops:
  42.6 1.6 %copy-start = (f32[2,256]{1,0:T(2,128)S(1)}, f32[2,256]{1,0:T(2,128)}, u32[]{:S(2)}) copy-start(f32[2,256]{1,0:T(2,128)} %get-tuple-element.11) | copy-start | bytes 6148

commit v4 on v3

--- a/solution.py
+++ b/solution.py
@@ -133,6 +133,15 @@
 
     pl.semaphore_wait(barrier, len(peers))
 
+    def shows():
+        return [copy(pj_out, pj_in, 6 + i, (s, i)) for i in range(ND - 1)]
+
+    @pl.when(d == ND - 1)
+    def _():
+        for each in shows():
+            each.start()
+        pj_in[...] = shown
+
     started = []
     for i, peer in enumerate([(down, d), (s, higher), (down, higher)]):
         started.append(copy(own_mod, mod_in.at[i], 3 + i, peer))
@@ -147,15 +156,6 @@
     for i, (plane, peer) in enumerate(((1, (down, d)), (0, (up, d)))):
         started.append(copy(st, hp.at[plane], 15 + i, peer))
         started[-1].start()
-
-    def shows():
-        return [copy(pj_out, pj_in, 6 + i, (s, i)) for i in range(ND - 1)]
-
-    @pl.when(d == ND - 1)
-    def _():
-        for each in shows():
-            each.start()
-        pj_in[...] = shown
 
     block_sum = jnp.zeros((24, NY), F32)
     force_sum = jnp.zeros((24, NY), F32)

time: 45.1 us -> 44 us (0.976)
  Pallas kernels: 41.9 us -> 40.9 us
    pallas_call x1, Pallas kernels: 41.9 us -> 40.9 us  [body(): pl.pallas_call(kernel, out_shape=(jax.ShapeDtypeStruct((24, ROWS, NY), F3...]
where the time goes in v4:
time: 44 us; the launch traced here: 43.7 us
  Pallas kernels  40.9 us (93%)
  local copies, waits for them, and re-layouts  2.2 us (5%)
  between operations  0.65 us (1%)
    pallas_call x1, Pallas kernels, body(): pl.pallas_call(kernel, out_shape=(jax.ShapeDtypeStruct((24, ROWS, NY), F3...  40.9 us
    unnamed x4, local copies, waits for them, and re-layouts  2.2 us

profile of v4, /device:TPU:1, one launch (start us, length us, event | category | flops | bytes accessed | tf_op | source)
XLA Modules:
  0.0 43.7 jit_solution(1922719809179223299)
XLA Ops:
  0.6 40.9 %shard_map.95 = (f32[24,8,256]{2,1,0:T(8,128)}, f32[2,256]{1,0:T(2,128)}) custom-call(f32[24,8,256]{2,1,0:T(8,128)} %bitcast.7, f32[3,8,256]{2,1,0:T(8,128)} %bitcast.8, s32[8,256]{1,0:T(8,128)} %bitcast.9, f32[16]{0:T(128)} %mod_ref.1, f32[24,24]{1,0:T(8,128)} %e_hbm.1, f32[384,384]{1,0:T(8,128)} %c_hbm.1, s32[1,256]{1,0:T(1,128)} %map_hbm.1, ...), custom_call_target="tpu_custom_call" | custom-call | tf_op jit(solution)/shard_map/pallas_call | solution.py:457
  41.5 0.0 copy-start
  41.5 1.6 %copy.13 = f32[3,8,1,8,256]{4,3,2,1,0:T(8,128)} copy(f32[3,8,1,8,256]{4,3,2,1,0:T(8,128)} %bitcast.6) | data formatting | bytes 393216
  43.2 0.0 copy-done
  43.2 0.6 %copy.14 = f32[2,256]{1,0:T(2,128)} copy(f32[2,256]{1,0:T(2,128)S(1)} %copy-done) | data formatting | bytes 4096
Async XLA Ops:
  41.5 1.6 %copy-start = (f32[2,256]{1,0:T(2,128)S(1)}, f32[2,256]{1,0:T(2,128)}, u32[]{:S(2)}) copy-start(f32[2,256]{1,0:T(2,128)} %get-tuple-element.11) | copy-start | bytes 6148
